TPU v7x, 32 devices: a whole 2x2x4 slice. The times are simulated.
32 devices in a mesh: groups: 2 (over y), tm: 16 (over z, x, core).
Axes of the slice: x: 2, y: 2, z: 4, core: 2. Of those that a mesh axis runs over, the one named last changes fastest.
Arguments:
- frames: bfloat16 [4096, 8192], P('tm', 'groups'), parts along dimension 1, may hold values from -6 to 6
- frame_valid: int32 [8192], P(('groups', 'tm')), parts along dimension 0, may hold values 0 or 1
- valid_count: int32 [32], P('groups'), parts along dimension 0, may hold values from 32 to 128, as said below
- block_map: int32 [32, 256], P('groups'), parts along dimension 0, may hold values from 0 to 255, as said below
- offsets: int32 [4, 2], replicated, may hold values from -4 to 4
Outputs:
- cross: float32 [512, 4, 2, 2048], P(('groups', 'tm')), parts along dimension 0
There are 2 independent parts, one for each index of `groups`. A program takes and returns all parts, laid end to end along the dimension named above; an argument that names none is the same for every part. Nothing has to cross between parts.
Inputs may be any that keep to these rules, and one draw needn't show every extreme that they name: `valid_count`: at most half of a tile's pixels are valid. Some tile has exactly 128 valid pixels and another exactly 32 in every draw; the others are spread evenly between the two. `block_map`: each row is a permutation of the pixels of a tile. Row steps lie in -4 to 4.
All inputs are finite; a program needn't handle non-finite values. No bound on the sum of `frame_valid` on one device may be relied on, other than what follows from the above.
Results may differ from a plain program's by a relative error of at most 0.0052.
Values may be sent and summed in bfloat16 or wider, within the bound.
A program may use at most 64 MiB of HBM per device.

v0:
```python
import functools
import math

import jax
import jax.numpy as jnp
import ml_dtypes
import numpy as np
from jax import lax
from jax.experimental import pallas as pl
from jax.experimental.pallas import tpu as pltpu
from jax.sharding import PartitionSpec as P

ROWS = 16
REACH = 4
RADIX = 16
VMEM_LIMIT = 56 * 1024 * 1024


def dft_table(frames_len):
    span = frames_len // RADIX
    per = span // 2
    j = np.arange(span)
    out = np.zeros((RADIX, 2 * per, 2 * span), np.float64)
    for k1 in range(RADIX):
        bins = k1 + RADIX * np.arange(per)
        angle = (bins[:, None] * j[None, :] % frames_len) * (2.0 * math.pi / frames_len)
        cos, sin = np.cos(angle), np.sin(angle)
        sign = 1.0 if k1 <= RADIX // 2 else -1.0
        out[k1, :per, :span] = cos
        out[k1, :per, span:] = sign * sin
        out[k1, per:, :span] = -sin
        out[k1, per:, span:] = sign * cos
    return (out / math.sqrt(frames_len)).astype(np.float32).astype(ml_dtypes.bfloat16)


def bits(flags):
    return flags.astype(jnp.float32).astype(jnp.bfloat16)


def dot_last(left, right):
    return lax.dot_general(
        left, right, (((1,), (1,)), ((), ())), preferred_element_type=jnp.float32
    )


def number_slots(count_ref, map_ref, slots_ref):
    tiles, tile_pix = map_ref.shape
    width = tile_pix // ROWS
    shift = width.bit_length() - 1
    group = tile_pix // ROWS
    row_idx = lax.broadcasted_iota(jnp.int32, (tile_pix, tile_pix), 0)
    col_idx = lax.broadcasted_iota(jnp.int32, (tile_pix, tile_pix), 1)
    row_high, row_low = row_idx >> shift, row_idx & (width - 1)
    col_high, col_low = col_idx >> shift, col_idx & (width - 1)
    same_tile = row_high == col_high
    same_low = bits(row_low == col_low)
    row_match = row_low == col_high
    before = bits(row_low * ROWS + row_high < col_low * ROWS + col_high)
    slim = lax.broadcasted_iota(jnp.int32, (group, tile_pix), 0)
    lane = lax.broadcasted_iota(jnp.int32, (group, tile_pix), 1)
    tile_pick = bits((lane >> shift) == slim)
    part_idx = lax.broadcasted_iota(jnp.int32, (group, ROWS, tile_pix), 1)
    for first in range(0, tiles, group):
        count = count_ref[first:first + group, :]
        pixel = map_ref[first:first + group, :]
        row = jnp.where(lane < count, pixel >> shift, -1)
        col = pixel & (width - 1)
        row_hot = (row[:, None, :] == part_idx).astype(jnp.float32).reshape(tile_pix, tile_pix)
        col_hot = (col[:, None, :] == part_idx).astype(jnp.float32).reshape(tile_pix, tile_pix)
        met = dot_last(row_hot.astype(jnp.bfloat16), col_hot.astype(jnp.bfloat16))
        met = jnp.where(same_tile, met, 0.0).astype(jnp.bfloat16)
        wide = jnp.dot(met, same_low, preferred_element_type=jnp.float32)
        wide = jnp.where(row_match, wide, 0.0).astype(jnp.bfloat16)
        valid = jnp.dot(tile_pick, wide, preferred_element_type=jnp.float32)
        rank = jnp.dot(valid.astype(jnp.bfloat16), before, preferred_element_type=jnp.float32)
        back = jnp.where((lane & (width - 1)) >= width // 2, tile_pix // 2 - count, 0)
        slots_ref[first:first + group, :] = jnp.where(
            valid > 0.5, rank.astype(jnp.int32) + back, -1
        )


def pick_pairs(me, tiles, slots_ref, offsets_ref, pick_ref, scale_ref):
    tile_pix = slots_ref.shape[1]
    width = tile_pix // ROWS
    shift = width.bit_length() - 1
    quarter = tile_pix // 4
    left = slots_ref[pl.ds((me + tiles - 1) % tiles, 1), :]
    own = slots_ref[pl.ds(me, 1), :]
    right = slots_ref[pl.ds((me + 1) % tiles, 1), :]
    left = jnp.where((left >= quarter * 1) & (me > 0), left + quarter, -1)
    right = jnp.where((right >= 0) & (right < quarter) & (me < tiles - 1), right + 3 * quarter, -1)
    row_idx = lax.broadcasted_iota(jnp.int32, (tile_pix, tile_pix), 0)
    col_idx = lax.broadcasted_iota(jnp.int32, (tile_pix, tile_pix), 1)
    sides = [bits(row_idx == ids) for ids in (left, own, right)]
    own_valid = None
    for which in range(5):
        row, col = row_idx >> shift, row_idx & (width - 1)
        if which > 0:
            row = row + offsets_ref[which - 1, 0]
            col = col + offsets_ref[which - 1, 1]
        here = ((row * width + (col & (width - 1))) == col_idx) & (row >= 0) & (row < ROWS)
        conds = (col < 0, (col >= 0) & (col < width), col >= width)
        found = None
        for cond, side in zip(conds, sides):
            term = dot_last(bits(here & cond), side)
            found = term if found is None else found + term
        pick_ref[which * tile_pix:(which + 1) * tile_pix, :] = found.astype(jnp.bfloat16)
        valid = jnp.sum(found, axis=1, keepdims=True)
        if which == 0:
            own_valid = valid
        else:
            both = jnp.broadcast_to(own_valid * valid, (tile_pix, 128)).reshape(ROWS, width, 128)
            scale_ref[which - 1] = 1.0 / jnp.maximum(jnp.sum(both, axis=0), 1.0)


def exchange_kernel(tiles, frames_ref, keep_ref, count_ref, map_ref, offsets_ref,
                    own_ref, left_ref, right_ref, pick_ref, scale_ref,
                    slots_ref, pack_ref, side_ref, send_sem, recv_sem, halo_send, halo_recv):
    me = lax.axis_index("tm")
    group = lax.axis_index("groups")
    rows = pack_ref.shape[1]
    slot_count = pack_ref.shape[2]
    tile_pix = slots_ref.shape[1]
    half_tiles = tiles // 2
    half = slot_count // 2
    mesh_id = pl.DeviceIdType.MESH

    barrier = pltpu.get_barrier_semaphore()

    def greet(step, carry):
        pl.semaphore_signal(
            barrier, inc=1, device_id=(group, (me + step) % tiles), device_id_type=mesh_id
        )
        return carry

    lax.fori_loop(1, tiles, greet, 0)

    number_slots(count_ref, map_ref, slots_ref)
    keep = jnp.broadcast_to(keep_ref[...].astype(jnp.float32), (slot_count, rows)).T
    slot_idx = lax.broadcasted_iota(jnp.int32, (slot_count, tile_pix), 0)

    def packed(tile):
        pick = bits(slot_idx == slots_ref[pl.ds(tile, 1), :])
        start = pl.multiple_of(tile * tile_pix, tile_pix)
        return (dot_last(frames_ref[:, pl.ds(start, tile_pix)], pick) * keep).astype(jnp.bfloat16)

    def block(source):
        return pl.ds(pl.multiple_of(source * rows, rows), rows)

    def to_owner(tile, source):
        return pltpu.make_async_remote_copy(
            src_ref=pack_ref.at[tile], dst_ref=own_ref.at[block(source)],
            send_sem=send_sem.at[tile], recv_sem=recv_sem.at[source],
            device_id=(group, tile), device_id_type=mesh_id,
        )

    pl.semaphore_wait(barrier, tiles - 1)

    def send(tile):
        pack_ref[tile] = packed(tile)
        to_owner(tile, me).start()

    send((me + half_tiles) % tiles)

    def send_two(step, carry):
        send((me + half_tiles + step) % tiles)
        send((me + step) % tiles)
        return carry

    lax.fori_loop(1, half_tiles, send_two, 0)
    own_ref[block(me), :] = packed(me)
    pick_pairs(me, tiles, slots_ref, offsets_ref, pick_ref, scale_ref)

    def to_side(way, source):
        target = (me + tiles - 1) % tiles if way == 0 else (me + 1) % tiles
        dst = right_ref if way == 0 else left_ref
        return pltpu.make_async_remote_copy(
            src_ref=side_ref.at[way, block(source)], dst_ref=dst.at[block(source)],
            send_sem=halo_send.at[way, source], recv_sem=halo_recv.at[way, source],
            device_id=(group, target), device_id_type=mesh_id,
        )

    has_left, has_right = me > 0, me < tiles - 1

    def forward(step, carry):
        low = (me + tiles - step) % half_tiles
        high = low + half_tiles
        for source in (low, high):
            @pl.when(source != me)
            def _():
                to_owner((me + 1) % tiles, source).wait_recv()
        near, far = own_ref[block(low), :], own_ref[block(high), :]
        side_ref[0, block(low), :] = jnp.concatenate([near[:, :half], far[:, :half]], axis=1)
        side_ref[1, block(low), :] = jnp.concatenate([near[:, half:], far[:, half:]], axis=1)

        @pl.when(has_left)
        def _():
            to_side(0, low).start()

        @pl.when(has_right)
        def _():
            to_side(1, low).start()

        return carry

    lax.fori_loop(0, half_tiles, forward, 0)

    @pl.when(me == 0)
    def _():
        left_ref[...] = jnp.zeros_like(left_ref)

    @pl.when(me == tiles - 1)
    def _():
        right_ref[...] = jnp.zeros_like(right_ref)

    def sent(step, carry):
        to_owner((me + step) % tiles, me).wait_send()
        return carry

    lax.fori_loop(1, tiles, sent, 0)

    def arrived(source, carry):
        @pl.when(has_left)
        def _():
            to_side(0, source).wait_send()
            to_side(1, source).wait_recv()

        @pl.when(has_right)
        def _():
            to_side(1, source).wait_send()
            to_side(0, source).wait_recv()

        return carry

    lax.fori_loop(0, half_tiles, arrived, 0)


def radix_sixteen(x):
    c1, c2, c3 = (math.cos(math.pi * n / 8.0) for n in (1, 2, 3))
    s = [x[d] + x[d + 8] for d in range(8)]
    t = [x[d] - x[d + 8] for d in range(8)]
    u = [s[d] + s[d + 4] for d in range(4)]
    v = [s[d] - s[d + 4] for d in range(4)]
    z = [None] * 9
    z[0] = (u[0] + u[2] + (u[1] + u[3]), None)
    z[8] = (u[0] + u[2] - (u[1] + u[3]), None)
    z[4] = (u[0] - u[2], u[3] - u[1])
    less, more = c2 * (v[1] - v[3]), c2 * (v[1] + v[3])
    z[2] = (v[0] + less, -(v[2] + more))
    z[6] = (v[0] - less, v[2] - more)
    a1, a2, a3 = t[1] - t[7], c2 * (t[2] - t[6]), t[3] - t[5]
    b1, b2, b3 = t[1] + t[7], c2 * (t[2] + t[6]), t[3] + t[5]
    p, q = t[0] + a2, c1 * a1 + c3 * a3
    z[1], z[7] = [p + q, None], [p - q, None]
    p, q = t[0] - a2, c3 * a1 - c1 * a3
    z[3], z[5] = [p + q, None], [p - q, None]
    p, q = c3 * b1 + c1 * b3, b2 + t[4]
    z[1][1], z[7][1] = -(p + q), q - p
    p, q = c1 * b1 - c3 * b3, b2 - t[4]
    z[3][1], z[5][1] = -(p + q), q - p
    return z


def cross_kernel(own_ref, left_ref, right_ref, table_ref, pick_ref, scale_ref, out_ref,
                 high_ref, spec_ref):
    frames_len, slot_count = own_ref.shape
    span = frames_len // RADIX
    per = span // 2
    step_rows = 16
    half = slot_count // 2

    lane = lax.broadcasted_iota(jnp.int32, (step_rows, slot_count), 1)
    front = lane < half

    def put(k1, part, start, lane0, value):
        if value is not None:
            rows = pl.ds(part * span + start, step_rows)
            high_ref[k1, rows, lane0:lane0 + slot_count] = value.astype(jnp.bfloat16)

    def one_step(step, carry):
        start = pl.multiple_of(step * step_rows, step_rows)
        own, near = [], [None] * RADIX
        for d in range(RADIX):
            own.append(own_ref[pl.ds(d * span + start, step_rows), :].astype(jnp.float32))
        for d in range(RADIX // 2):
            left = left_ref[pl.ds(d * span + start, step_rows), :].astype(jnp.float32)
            right = right_ref[pl.ds(d * span + start, step_rows), :].astype(jnp.float32)
            near[d] = jnp.where(front, left, pltpu.roll(right, half, 1))
            near[d + 8] = jnp.where(front, pltpu.roll(left, half, 1), right)
        for lane0, group in ((0, own), (slot_count, near)):
            for k1, (real, imag) in enumerate(radix_sixteen(group)):
                put(k1, 0, start, lane0, real)
                put(k1, 1, start, lane0, imag)
        return carry

    lax.fori_loop(0, span // step_rows, one_step, 0)

    for k1 in range(RADIX):
        src = min(k1, RADIX - k1)
        depth = span if k1 % (RADIX // 2) == 0 else 2 * span
        found = jnp.dot(
            table_ref[k1, :, :depth], high_ref[src, :depth, :], preferred_element_type=jnp.float32
        )
        for side in range(2):
            lanes = slice(side * slot_count, (side + 1) * slot_count)
            for part in range(2):
                spec_ref[part, side, pl.ds(k1, per, RADIX), :] = found[part * per:(part + 1) * per, lanes]

    bins = RADIX * per
    width = 256
    pix = pick_ref.shape[0] // 5
    cols = pix // ROWS

    def one_band(band, carry):
        start = pl.multiple_of(band * width, width)
        grids = []
        for part in range(2):
            spec = jnp.concatenate(
                [spec_ref[part, side, pl.ds(start, width), :] for side in range(2)], axis=1
            ).astype(jnp.bfloat16)
            grids.append(lax.dot_general(
                pick_ref[...], spec, (((1,), (1,)), ((), ())), preferred_element_type=jnp.float32
            ))
        real, imag = grids
        own_r, own_i = real[:pix], imag[:pix]
        for which in range(4):
            rows = slice((which + 1) * pix, (which + 2) * pix)
            far_r, far_i = real[rows], imag[rows]
            scale = jnp.concatenate([scale_ref[which]] * (width // 128), axis=1)
            out_r = jnp.sum((own_r * far_r + own_i * far_i).reshape(ROWS, cols, width), axis=0)
            out_i = jnp.sum((own_i * far_r - own_r * far_i).reshape(ROWS, cols, width), axis=0)
            out_ref[:, which, 0, pl.ds(start, width)] = out_r * scale
            out_ref[:, which, 1, pl.ds(start, width)] = out_i * scale
        return carry

    lax.fori_loop(0, bins // width, one_band, 0)


def per_device(table, frames, frame_valid, valid_count, block_map, offsets):
    tile_count = lax.axis_size("tm")
    frame_dev, pixel_count = frames.shape
    tile_pix = pixel_count // tile_count
    tile_width = tile_pix // ROWS
    slot_count = tile_pix // 2
    frames_len = tile_count * frame_dev
    span = frames_len // RADIX
    bins = frames_len // 2
    vmem = pl.BlockSpec(memory_space=pltpu.VMEM)
    own, left, right, pick, scales = pl.pallas_call(
        functools.partial(exchange_kernel, tile_count),
        out_shape=[
            jax.ShapeDtypeStruct((frames_len, slot_count), jnp.bfloat16),
            jax.ShapeDtypeStruct((bins, slot_count), jnp.bfloat16),
            jax.ShapeDtypeStruct((bins, slot_count), jnp.bfloat16),
            jax.ShapeDtypeStruct((5 * tile_pix, tile_pix), jnp.bfloat16),
            jax.ShapeDtypeStruct((offsets.shape[0], tile_width, 128), jnp.float32),
        ],
        in_specs=[vmem] * 4 + [pl.BlockSpec(memory_space=pltpu.SMEM)],
        out_specs=[vmem] * 5,
        scratch_shapes=[
            pltpu.VMEM((tile_count, tile_pix), jnp.int32),
            pltpu.VMEM((tile_count, frame_dev, slot_count), jnp.bfloat16),
            pltpu.VMEM((2, bins, slot_count), jnp.bfloat16),
            pltpu.SemaphoreType.DMA((tile_count,)),
            pltpu.SemaphoreType.DMA((tile_count,)),
            pltpu.SemaphoreType.DMA((2, tile_count // 2)),
            pltpu.SemaphoreType.DMA((2, tile_count // 2)),
        ],
        compiler_params=pltpu.CompilerParams(
            vmem_limit_bytes=VMEM_LIMIT, collective_id=0, has_side_effects=True
        ),
        name="exchange",
    )(frames, frame_valid[None, :], valid_count[:, None], block_map, offsets)
    return pl.pallas_call(
        cross_kernel,
        out_shape=jax.ShapeDtypeStruct((tile_width, offsets.shape[0], 2, bins), jnp.float32),
        scratch_shapes=[
            pltpu.VMEM((RADIX // 2 + 1, 2 * span, 2 * slot_count), jnp.bfloat16),
            pltpu.VMEM((2, 2, bins, slot_count), jnp.float32),
        ],
        compiler_params=pltpu.CompilerParams(vmem_limit_bytes=VMEM_LIMIT),
        name="transform_cross",
    )(own, left, right, table, pick, scales)


def solution(mesh):
    def run(frames, frame_valid, valid_count, block_map, offsets):
        table = jnp.asarray(dft_table(frames.shape[0]))
        return jax.shard_map(
            per_device,
            mesh=mesh,
            in_specs=(P(), P("tm", "groups"), P(("groups", "tm")), P("groups"), P("groups", None), P()),
            out_specs=P(("groups", "tm"), None, None, None),
            check_vma=False,
        )(table, frames, frame_valid, valid_count, block_map, offsets)

    return run
```

profile of v0, /device:TPU:10, one launch (start us, length us, event | category | flops | bytes accessed | tf_op | source)
XLA Modules:
  0.0 54.8 jit_solution(2540276920895056637)
XLA Ops:
  0.0 1.3 %copy.8.offsets_ref = s32[4,2]{1,0:T(4,128)} copy(s32[4,2]{0,1:T(2,128)} %param.10) | data formatting | bytes 64 | tf_op args[4]
  1.3 1.3 %copy.7.count_ref = s32[16,1]{1,0:T(8,128)} copy(s32[16,1]{0,1:T(1,128)} %bitcast.3) | data formatting | bytes 128 | tf_op jit(solution)/shard_map/broadcast_in_dim | solution.py:373
  2.7 39.4 %exchange.1 = (bf16[4096,128]{1,0:T(8,128)(2,1)}, bf16[2048,128]{1,0:T(8,128)(2,1)}, bf16[2048,128]{1,0:T(8,128)(2,1)}, bf16[1280,256]{1,0:T(8,128)(2,1)}, f32[4,16,128]{2,1,0:T(8,128)}) custom-call(bf16[256,4096]{1,0:T(8,128)(2,1)} %frames_ref.1, s32[1,256]{1,0:T(1,128)} %bitcast.2, s32[16,1]{1,0:T(8,128)} %copy.7.count_ref, s32[16,256]{1,0:T(8,128)} %map_ref.1, ...), custom_call_target="tpu_custom_call" | custom-call | tf_op jit(solution)/shard_map/exchange/pallas_call | solution.py:349
  42.1 12.7 %transform_cross.1 = f32[16,4,2,2048]{3,2,1,0:T(2,128)} custom-call(bf16[4096,128]{1,0:T(8,128)(2,1)} %get-tuple-element.10.own_ref, bf16[2048,128]{1,0:T(8,128)(2,1)} %get-tuple-element.11.left_ref, bf16[2048,128]{1,0:T(8,128)(2,1)} %get-tuple-element.12.right_ref, bf16[16,256,512]{2,1,0:T(8,128)(2,1)} %constant.2.clone.table_ref, ...), custom_call_target="tpu_custom_call" | custom-call | tf_op jit(solution)/shard_map/transform_cross/pallas_call | solution.py:374
where the time goes:
time: 55 us; the launch traced here: 54.8 us
  Pallas kernels  52.1 us (95%)
  local copies, waits for them, and re-layouts  2.67 us (5%)
    pallas_call x1, Pallas kernels, per_device(): pl.pallas_call(functools.partial(exchange_kernel, tile_count), out_shape=...  39.4 us
    pallas_call x1, Pallas kernels, per_device(): pl.pallas_call(cross_kernel, out_shape=jax.ShapeDtypeStruct((tile_width,...  12.7 us
    unnamed x1, local copies, waits for them, and re-layouts  1.35 us
    broadcast_in_dim x1, local copies, waits for them, and re-layouts, per_device(): valid_count[:, None]  1.33 us

commit v1 on v0

--- a/solution.py
+++ b/solution.py
@@ -13,7 +13,8 @@
 ROWS = 16
 REACH = 4
 RADIX = 16
-VMEM_LIMIT = 56 * 1024 * 1024
+EXCHANGE_VMEM = 24 * 1024 * 1024
+CROSS_VMEM = 36 * 1024 * 1024
 
 
 def dft_table(frames_len):
@@ -61,7 +62,12 @@
     tile_pick = bits((lane >> shift) == slim)
     part_idx = lax.broadcasted_iota(jnp.int32, (group, ROWS, tile_pix), 1)
     for first in range(0, tiles, group):
-        count = count_ref[first:first + group, :]
+        near_diag = lax.broadcasted_iota(jnp.int32, (group, tiles), 1) == (
+            lax.broadcasted_iota(jnp.int32, (group, tiles), 0) + first
+        )
+        count = jnp.sum(
+            jnp.where(near_diag, count_ref[...].astype(jnp.float32), 0.0), axis=1, keepdims=True
+        ).astype(jnp.int32)
         pixel = map_ref[first:first + group, :]
         row = jnp.where(lane < count, pixel >> shift, -1)
         col = pixel & (width - 1)
@@ -96,8 +102,8 @@
     for which in range(5):
         row, col = row_idx >> shift, row_idx & (width - 1)
         if which > 0:
-            row = row + offsets_ref[which - 1, 0]
-            col = col + offsets_ref[which - 1, 1]
+            row = row + offsets_ref[0:1, which - 1:which]
+            col = col + offsets_ref[1:2, which - 1:which]
         here = ((row * width + (col & (width - 1))) == col_idx) & (row >= 0) & (row < ROWS)
         conds = (col < 0, (col >= 0) & (col < width), col >= width)
         found = None
@@ -115,7 +121,8 @@
 
 def exchange_kernel(tiles, frames_ref, keep_ref, count_ref, map_ref, offsets_ref,
                     own_ref, left_ref, right_ref, pick_ref, scale_ref,
-                    slots_ref, pack_ref, side_ref, send_sem, recv_sem, halo_send, halo_recv):
+                    slots_ref, pack_ref, side_ref, fold_ref, direct_ref,
+                    send_sem, recv_sem, halo_send, halo_recv, direct_send, direct_recv):
     me = lax.axis_index("tm")
     group = lax.axis_index("groups")
     rows = pack_ref.shape[1]
@@ -168,7 +175,33 @@
         return carry
 
     lax.fori_loop(1, half_tiles, send_two, 0)
-    own_ref[block(me), :] = packed(me)
+    pack_ref[me] = packed(me)
+    own_ref[block(me), :] = pack_ref[me]
+
+    mid = half_tiles - 1
+    mids = (mid, mid + 1)
+
+    def to_mid(which, source):
+        return pltpu.make_async_remote_copy(
+            src_ref=fold_ref.at[which], dst_ref=direct_ref.at[source],
+            send_sem=direct_send.at[which], recv_sem=direct_recv.at[source],
+            device_id=(group, mids[which]), device_id_type=mesh_id,
+        )
+
+    for which in range(2):
+        block_there = pack_ref[mids[1 - which]]
+        lanes = slice(0, half) if which == 0 else slice(half, slot_count)
+        margin = block_there[:, lanes]
+        fold_ref[which] = jnp.concatenate([margin[:rows // 2], margin[rows // 2:]], axis=1)
+
+        @pl.when(me != mids[which])
+        def _():
+            to_mid(which, me).start()
+
+        @pl.when(me == mids[which])
+        def _():
+            direct_ref[me] = fold_ref[which]
+
     pick_pairs(me, tiles, slots_ref, offsets_ref, pick_ref, scale_ref)
 
     def to_side(way, source):
@@ -180,7 +213,8 @@
             device_id=(group, target), device_id_type=mesh_id,
         )
 
-    has_left, has_right = me > 0, me < tiles - 1
+    has_left = (me > 0) & (me != half_tiles)
+    has_right = (me < tiles - 1) & (me != half_tiles - 1)
 
     def forward(step, carry):
         low = (me + tiles - step) % half_tiles
@@ -212,6 +246,26 @@
     @pl.when(me == tiles - 1)
     def _():
         right_ref[...] = jnp.zeros_like(right_ref)
+
+    for which, dst in ((0, right_ref), (1, left_ref)):
+        @pl.when(me == mids[which])
+        def _():
+            def unfold(low, carry):
+                parts = []
+                for source in (low, low + half_tiles):
+                    @pl.when(source != me)
+                    def _():
+                        to_mid(1 - which, source).wait_recv()
+                    fold = direct_ref[source]
+                    parts.append(jnp.concatenate([fold[:, :half], fold[:, half:]], axis=0))
+                dst[block(low), :] = jnp.concatenate(parts, axis=1)
+                return carry
+
+            lax.fori_loop(0, half_tiles, unfold, 0)
+
+        @pl.when(me != mids[which])
+        def _():
+            to_mid(which, me).wait_send()
 
     def sent(step, carry):
         to_owner((me + step) % tiles, me).wait_send()
@@ -355,22 +409,26 @@
             jax.ShapeDtypeStruct((5 * tile_pix, tile_pix), jnp.bfloat16),
             jax.ShapeDtypeStruct((offsets.shape[0], tile_width, 128), jnp.float32),
         ],
-        in_specs=[vmem] * 4 + [pl.BlockSpec(memory_space=pltpu.SMEM)],
+        in_specs=[vmem] * 5,
         out_specs=[vmem] * 5,
         scratch_shapes=[
             pltpu.VMEM((tile_count, tile_pix), jnp.int32),
             pltpu.VMEM((tile_count, frame_dev, slot_count), jnp.bfloat16),
             pltpu.VMEM((2, bins, slot_count), jnp.bfloat16),
+            pltpu.VMEM((2, frame_dev // 2, slot_count), jnp.bfloat16),
+            pltpu.VMEM((tile_count, frame_dev // 2, slot_count), jnp.bfloat16),
             pltpu.SemaphoreType.DMA((tile_count,)),
             pltpu.SemaphoreType.DMA((tile_count,)),
             pltpu.SemaphoreType.DMA((2, tile_count // 2)),
             pltpu.SemaphoreType.DMA((2, tile_count // 2)),
+            pltpu.SemaphoreType.DMA((2,)),
+            pltpu.SemaphoreType.DMA((tile_count,)),
         ],
         compiler_params=pltpu.CompilerParams(
-            vmem_limit_bytes=VMEM_LIMIT, collective_id=0, has_side_effects=True
+            vmem_limit_bytes=EXCHANGE_VMEM, collective_id=0, has_side_effects=True
         ),
         name="exchange",
-    )(frames, frame_valid[None, :], valid_count[:, None], block_map, offsets)
+    )(frames, frame_valid[None, :], valid_count[None, :], block_map, offsets.T)
     return pl.pallas_call(
         cross_kernel,
         out_shape=jax.ShapeDtypeStruct((tile_width, offsets.shape[0], 2, bins), jnp.float32),
@@ -378,7 +436,7 @@
             pltpu.VMEM((RADIX // 2 + 1, 2 * span, 2 * slot_count), jnp.bfloat16),
             pltpu.VMEM((2, 2, bins, slot_count), jnp.float32),
         ],
-        compiler_params=pltpu.CompilerParams(vmem_limit_bytes=VMEM_LIMIT),
+        compiler_params=pltpu.CompilerParams(vmem_limit_bytes=CROSS_VMEM),
         name="transform_cross",
     )(own, left, right, table, pick, scales)
 

time: 55 us -> 51.2 us (0.931)
  the two profiles are of different devices: /device:TPU:10 before, /device:TPU:22 now
where the time goes in v1:
time: 51.2 us; the launch traced here: 50.9 us
  Pallas kernels  44.4 us (87%)
  local copies, waits for them, and re-layouts  6.5 us (13%)
    pallas_call x1, Pallas kernels, per_device(): pl.pallas_call(functools.partial(exchange_kernel, tile_count), out_shape=...  34.7 us
    pallas_call x1, Pallas kernels, per_device(): pl.pallas_call(cross_kernel, out_shape=jax.ShapeDtypeStruct((tile_width,...  9.68 us
    unnamed x12, local copies, waits for them, and re-layouts  6.5 us

profile of v1, /device:TPU:22, one launch (start us, length us, event | category | flops | bytes accessed | tf_op | source)
XLA Modules:
  0.0 50.9 jit_solution(9788467216305423544)
XLA Ops:
  0.0 0.0 copy-start.1
  0.0 1.6 %copy-done.1 = bf16[256,4096]{1,0:T(8,128)(2,1)S(1)} copy-done((bf16[256,4096]{1,0:T(8,128)(2,1)S(1)}, bf16[256,4096]{1,0:T(8,128)(2,1)}, u32[]{:S(2)}) %copy-start.1) | copy-done | bytes 2097176
  1.6 0.0 copy-start.2
  1.6 0.7 %copy-done.2 = s32[16,256]{1,0:T(8,128)S(1)} copy-done((s32[16,256]{1,0:T(8,128)S(1)}, s32[16,256]{1,0:T(8,128)}, u32[]{:S(2)}) %copy-start.2) | copy-done | bytes 16408
  2.3 0.0 copy-start.3
  2.3 0.7 %copy-done.3 = s32[256]{0:T(256)S(1)} copy-done((s32[256]{0:T(256)S(1)}, s32[256]{0:T(256)}, u32[]{:S(2)}) %copy-start.3) | copy-done | bytes 1048
  3.0 0.0 copy-start.4
  3.0 0.7 %copy-done.4 = s32[4,2]{0,1:T(2,128)S(1)} copy-done((s32[4,2]{0,1:T(2,128)S(1)}, s32[4,2]{0,1:T(2,128)}, u32[]{:S(2)}) %copy-start.4) | copy-done | bytes 56
  3.7 0.0 copy-start.5
  3.7 0.7 %copy-done.5 = s32[16]{0:T(128)S(1)} copy-done((s32[16]{0:T(128)S(1)}, s32[16]{0:T(128)}, u32[]{:S(2)}) %copy-start.5) | copy-done | bytes 88
  4.3 34.7 %exchange.1 = (bf16[4096,128]{1,0:T(8,128)(2,1)S(1)}, bf16[2048,128]{1,0:T(8,128)(2,1)S(1)}, bf16[2048,128]{1,0:T(8,128)(2,1)S(1)}, bf16[1280,256]{1,0:T(8,128)(2,1)S(1)}, f32[4,16,128]{2,1,0:T(8,128)S(1)}) custom-call(bf16[256,4096]{1,0:T(8,128)(2,1)S(1)} %copy-done.1, s32[1,256]{1,0:T(1,128)S(1)} %bitcast.3, s32[1,16]{1,0:T(1,128)S(1)} %bitcast.5, ...), custom_call_target="tpu_custom_call" | custom-call | tf_op jit(solution)/shard_map/exchange/pallas_call | solution.py:403
  39.0 0.0 copy-start
  39.0 2.2 %copy-done = bf16[16,256,512]{2,1,0:T(8,128)(2,1)S(1)} copy-done((bf16[16,256,512]{2,1,0:T(8,128)(2,1)S(1)}, bf16[16,256,512]{2,1,0:T(8,128)(2,1)}, u32[]{:S(2)}) %copy-start) | copy-done | bytes 4194328
  41.2 9.7 %transform_cross.1 = f32[16,4,2,2048]{3,2,1,0:T(2,128)} custom-call(bf16[4096,128]{1,0:T(8,128)(2,1)S(1)} %get-tuple-element.10.own_ref, bf16[2048,128]{1,0:T(8,128)(2,1)S(1)} %get-tuple-element.11.left_ref, bf16[2048,128]{1,0:T(8,128)(2,1)S(1)} %get-tuple-element.12.right_ref, bf16[16,256,512]{2,1,0:T(8,128)(2,1)S(1)} %copy-done, ...), custom_call_target="tpu_custom_call" | custom-call | tf_op jit(solution)/shard_map/transform_cross/pallas_call | solution.py:432
Async XLA Ops:
  0.0 1.6 %copy-start.1 = (bf16[256,4096]{1,0:T(8,128)(2,1)S(1)}, bf16[256,4096]{1,0:T(8,128)(2,1)}, u32[]{:S(2)}) copy-start(bf16[256,4096]{1,0:T(8,128)(2,1)} %frames_ref.1) | copy-start | bytes 6291460
  1.6 0.7 %copy-start.2 = (s32[16,256]{1,0:T(8,128)S(1)}, s32[16,256]{1,0:T(8,128)}, u32[]{:S(2)}) copy-start(s32[16,256]{1,0:T(8,128)} %map_ref.1) | copy-start | bytes 49156
  2.3 0.7 %copy-start.3 = (s32[256]{0:T(256)S(1)}, s32[256]{0:T(256)}, u32[]{:S(2)}) copy-start(s32[256]{0:T(256)} %param.7) | copy-start | bytes 3076
  3.0 0.7 %copy-start.4 = (s32[4,2]{0,1:T(2,128)S(1)}, s32[4,2]{0,1:T(2,128)}, u32[]{:S(2)}) copy-start(s32[4,2]{0,1:T(2,128)} %param.10) | copy-start | bytes 100
  3.7 0.7 %copy-start.5 = (s32[16]{0:T(128)S(1)}, s32[16]{0:T(128)}, u32[]{:S(2)}) copy-start(s32[16]{0:T(128)} %param.8) | copy-start | bytes 196
  39.0 2.2 %copy-start = (bf16[16,256,512]{2,1,0:T(8,128)(2,1)S(1)}, bf16[16,256,512]{2,1,0:T(8,128)(2,1)}, u32[]{:S(2)}) copy-start(bf16[16,256,512]{2,1,0:T(8,128)(2,1)} %constant.2.clone.table_ref) | copy-start | bytes 12582916

commit v2 on v1

--- a/solution.py
+++ b/solution.py
@@ -13,8 +13,7 @@
 ROWS = 16
 REACH = 4
 RADIX = 16
-EXCHANGE_VMEM = 24 * 1024 * 1024
-CROSS_VMEM = 36 * 1024 * 1024
+VMEM_LIMIT = 56 * 1024 * 1024
 
 
 def dft_table(frames_len):
@@ -119,10 +118,11 @@
             scale_ref[which - 1] = 1.0 / jnp.maximum(jnp.sum(both, axis=0), 1.0)
 
 
-def exchange_kernel(tiles, frames_ref, keep_ref, count_ref, map_ref, offsets_ref,
+def exchange_kernel(tiles, far_ref, keep_ref, count_ref, map_ref, offsets_ref,
                     own_ref, left_ref, right_ref, pick_ref, scale_ref,
-                    slots_ref, pack_ref, side_ref, fold_ref, direct_ref,
-                    send_sem, recv_sem, halo_send, halo_recv, direct_send, direct_recv):
+                    frames_ref, slots_ref, pack_ref, side_ref, fold_ref, direct_ref,
+                    send_sem, recv_sem, halo_send, halo_recv, direct_send, direct_recv,
+                    load_sem):
     me = lax.axis_index("tm")
     group = lax.axis_index("groups")
     rows = pack_ref.shape[1]
@@ -132,6 +132,8 @@
     half = slot_count // 2
     mesh_id = pl.DeviceIdType.MESH
 
+    load = pltpu.make_async_copy(far_ref, frames_ref, load_sem)
+    load.start()
     barrier = pltpu.get_barrier_semaphore()
 
     def greet(step, carry):
@@ -161,6 +163,7 @@
             device_id=(group, tile), device_id_type=mesh_id,
         )
 
+    load.wait()
     pl.semaphore_wait(barrier, tiles - 1)
 
     def send(tile):
@@ -315,8 +318,10 @@
     return z
 
 
-def cross_kernel(own_ref, left_ref, right_ref, table_ref, pick_ref, scale_ref, out_ref,
-                 high_ref, spec_ref):
+def cross_kernel(own_ref, left_ref, right_ref, far_ref, pick_ref, scale_ref, out_ref,
+                 high_ref, spec_ref, table_ref, load_sem):
+    load = pltpu.make_async_copy(far_ref, table_ref, load_sem)
+    load.start()
     frames_len, slot_count = own_ref.shape
     span = frames_len // RADIX
     per = span // 2
@@ -349,6 +354,7 @@
 
     lax.fori_loop(0, span // step_rows, one_step, 0)
 
+    load.wait()
     for k1 in range(RADIX):
         src = min(k1, RADIX - k1)
         depth = span if k1 % (RADIX // 2) == 0 else 2 * span
@@ -387,7 +393,7 @@
             out_ref[:, which, 1, pl.ds(start, width)] = out_i * scale
         return carry
 
-    lax.fori_loop(0, bins // width, one_band, 0)
+    lax.fori_loop(0, bins // width, one_band, 0, unroll=4)
 
 
 def per_device(table, frames, frame_valid, valid_count, block_map, offsets):
@@ -409,9 +415,10 @@
             jax.ShapeDtypeStruct((5 * tile_pix, tile_pix), jnp.bfloat16),
             jax.ShapeDtypeStruct((offsets.shape[0], tile_width, 128), jnp.float32),
         ],
-        in_specs=[vmem] * 5,
+        in_specs=[pl.BlockSpec(memory_space=pl.ANY)] + [vmem] * 4,
         out_specs=[vmem] * 5,
         scratch_shapes=[
+            pltpu.VMEM((frame_dev, pixel_count), jnp.bfloat16),
             pltpu.VMEM((tile_count, tile_pix), jnp.int32),
             pltpu.VMEM((tile_count, frame_dev, slot_count), jnp.bfloat16),
             pltpu.VMEM((2, bins, slot_count), jnp.bfloat16),
@@ -423,9 +430,10 @@
             pltpu.SemaphoreType.DMA((2, tile_count // 2)),
             pltpu.SemaphoreType.DMA((2,)),
             pltpu.SemaphoreType.DMA((tile_count,)),
+            pltpu.SemaphoreType.DMA,
         ],
         compiler_params=pltpu.CompilerParams(
-            vmem_limit_bytes=EXCHANGE_VMEM, collective_id=0, has_side_effects=True
+            vmem_limit_bytes=VMEM_LIMIT, collective_id=0, has_side_effects=True
         ),
         name="exchange",
     )(frames, frame_valid[None, :], valid_count[None, :], block_map, offsets.T)
@@ -435,8 +443,12 @@
         scratch_shapes=[
             pltpu.VMEM((RADIX // 2 + 1, 2 * span, 2 * slot_count), jnp.bfloat16),
             pltpu.VMEM((2, 2, bins, slot_count), jnp.float32),
+            pltpu.VMEM(table.shape, table.dtype),
+            pltpu.SemaphoreType.DMA,
         ],
-        compiler_params=pltpu.CompilerParams(vmem_limit_bytes=CROSS_VMEM),
+        in_specs=[vmem] * 3 + [pl.BlockSpec(memory_space=pl.ANY)] + [vmem] * 2,
+        out_specs=vmem,
+        compiler_params=pltpu.CompilerParams(vmem_limit_bytes=VMEM_LIMIT),
         name="transform_cross",
     )(own, left, right, table, pick, scales)
 

time: 51.2 us -> 47.7 us (0.932)
  local copies, waits for them, and re-layouts: 6.5 us -> 0 us
  Pallas kernels: 44.4 us -> 47.4 us
    unnamed x12 -> x0, local copies, waits for them, and re-layouts: 6.5 us -> none
    pallas_call x1, Pallas kernels: 34.7 us -> 37.1 us  [per_device(): pl.pallas_call(functools.partial(exchange_kernel, tile_count), out_shape=...]
    pallas_call x1, Pallas kernels: 9.68 us -> 10.3 us  [per_device(): pl.pallas_call(cross_kernel, out_shape=jax.ShapeDtypeStruct((tile_width,...]
where the time goes in v2:
time: 47.7 us; the launch traced here: 47.5 us
  Pallas kernels  47.4 us (99%)
    pallas_call x1, Pallas kernels, per_device(): pl.pallas_call(functools.partial(exchange_kernel, tile_count), out_shape=...  37.1 us
    pallas_call x1, Pallas kernels, per_device(): pl.pallas_call(cross_kernel, out_shape=jax.ShapeDtypeStruct((tile_width,...  10.3 us

profile of v2, /device:TPU:22, one launch (start us, length us, event | category | flops | bytes accessed | tf_op | source)
XLA Modules:
  0.0 47.5 jit_solution(409052593105766215)
XLA Ops:
  0.0 37.1 %exchange.1 = (bf16[4096,128]{1,0:T(8,128)(2,1)}, bf16[2048,128]{1,0:T(8,128)(2,1)}, bf16[2048,128]{1,0:T(8,128)(2,1)}, bf16[1280,256]{1,0:T(8,128)(2,1)}, f32[4,16,128]{2,1,0:T(8,128)}) custom-call(bf16[256,4096]{1,0:T(8,128)(2,1)} %far_ref.2, s32[1,256]{1,0:T(1,128)} %bitcast.3, s32[1,16]{1,0:T(1,128)} %bitcast.5, s32[16,256]{1,0:T(8,128)} %map_ref.1, ...), custom_call_target="tpu_custom_call" | custom-call | tf_op jit(solution)/shard_map/exchange/pallas_call | solution.py:409
  37.1 10.3 %transform_cross.1 = f32[16,4,2,2048]{3,2,1,0:T(2,128)} custom-call(bf16[4096,128]{1,0:T(8,128)(2,1)} %get-tuple-element.10.own_ref, bf16[2048,128]{1,0:T(8,128)(2,1)} %get-tuple-element.11.left_ref, bf16[2048,128]{1,0:T(8,128)(2,1)} %get-tuple-element.12.right_ref, bf16[16,256,512]{2,1,0:T(8,128)(2,1)} %constant.2.clone.far_ref, ...), custom_call_target="tpu_custom_call" | custom-call | tf_op jit(solution)/shard_map/transform_cross/pallas_call | solution.py:440

commit v3 on v2

--- a/solution.py
+++ b/solution.py
@@ -116,6 +116,7 @@
         else:
             both = jnp.broadcast_to(own_valid * valid, (tile_pix, 128)).reshape(ROWS, width, 128)
             scale_ref[which - 1] = 1.0 / jnp.maximum(jnp.sum(both, axis=0), 1.0)
+        yield which
 
 
 def exchange_kernel(tiles, far_ref, keep_ref, count_ref, map_ref, offsets_ref,
@@ -205,7 +206,6 @@
         def _():
             direct_ref[me] = fold_ref[which]
 
-    pick_pairs(me, tiles, slots_ref, offsets_ref, pick_ref, scale_ref)
 
     def to_side(way, source):
         target = (me + tiles - 1) % tiles if way == 0 else (me + 1) % tiles
@@ -240,7 +240,12 @@
 
         return carry
 
-    lax.fori_loop(0, half_tiles, forward, 0)
+    started = 0
+    for _ in pick_pairs(me, tiles, slots_ref, offsets_ref, pick_ref, scale_ref):
+        if started < half_tiles:
+            forward(started, 0)
+            started += 1
+    lax.fori_loop(started, half_tiles, forward, 0)
 
     @pl.when(me == 0)
     def _():

time: 47.7 us -> 47.7 us (level)
  no operation moved by 1% of the time
where the time goes in v3:
time: 47.7 us; the launch traced here: 47.5 us
  Pallas kernels  47.4 us (99%)
    pallas_call x1, Pallas kernels, per_device(): pl.pallas_call(functools.partial(exchange_kernel, tile_count), out_shape=...  37.1 us
    pallas_call x1, Pallas kernels, per_device(): pl.pallas_call(cross_kernel, out_shape=jax.ShapeDtypeStruct((tile_width,...  10.3 us

profile of v3, /device:TPU:22, one launch (start us, length us, event | category | flops | bytes accessed | tf_op | source)
XLA Modules:
  0.0 47.5 jit_solution(15062249123805570531)
XLA Ops:
  0.0 37.1 %exchange.1 = (bf16[4096,128]{1,0:T(8,128)(2,1)}, bf16[2048,128]{1,0:T(8,128)(2,1)}, bf16[2048,128]{1,0:T(8,128)(2,1)}, bf16[1280,256]{1,0:T(8,128)(2,1)}, f32[4,16,128]{2,1,0:T(8,128)}) custom-call(bf16[256,4096]{1,0:T(8,128)(2,1)} %far_ref.2, s32[1,256]{1,0:T(1,128)} %bitcast.3, s32[1,16]{1,0:T(1,128)} %bitcast.5, s32[16,256]{1,0:T(8,128)} %map_ref.1, ...), custom_call_target="tpu_custom_call" | custom-call | tf_op jit(solution)/shard_map/exchange/pallas_call | solution.py:414
  37.1 10.3 %transform_cross.1 = f32[16,4,2,2048]{3,2,1,0:T(2,128)} custom-call(bf16[4096,128]{1,0:T(8,128)(2,1)} %get-tuple-element.10.own_ref, bf16[2048,128]{1,0:T(8,128)(2,1)} %get-tuple-element.11.left_ref, bf16[2048,128]{1,0:T(8,128)(2,1)} %get-tuple-element.12.right_ref, bf16[16,256,512]{2,1,0:T(8,128)(2,1)} %constant.2.clone.far_ref, ...), custom_call_target="tpu_custom_call" | custom-call | tf_op jit(solution)/shard_map/transform_cross/pallas_call | solution.py:445
